TPU v7x, 512 devices: a whole 4x4x16 slice. The times are simulated.
512 devices in a mesh: dp: 64 (over y, z), heads: 8 (over x, core).
Axes of the slice: x: 4, y: 4, z: 16, core: 2. Of those that a mesh axis runs over, the one named last changes fastest.
Arguments:
- queries: bfloat16 [64, 128, 8192], P('dp', 'heads'), may hold values from -14 to 14
- out_grad: bfloat16 [64, 128, 8192], P('dp', 'heads'), may hold values from -6 to 6
- keys: bfloat16 [64, 1792, 1024], P('dp', None, 'heads'), may hold values from -7 to 7
- values: bfloat16 [64, 1792, 1024], P('dp', None, 'heads'), may hold values from -4 to 4
- image_owner: int32 [64], replicated, may hold values from 0 to 63, each once
- tile_count: int32 [64], replicated, may hold values from 1 to 7, as said below
- seq_images: int32 [64, 2], replicated, may hold values from 0 to 63, as said below
- text_len: int32 [64], P('dp'), may hold values from 64 to 128, as said below
- tile_mask: int32 [64, 2, 7], P('dp'), may hold values from 0 to 1, as said below
Outputs:
- attn_out: bfloat16 [64, 128, 8192], P('dp', 'heads')
- query_grad: bfloat16 [64, 128, 8192], P('dp', 'heads')
- key_grad: bfloat16 [64, 1792, 1024], P('dp', None, 'heads')
- value_grad: bfloat16 [64, 1792, 1024], P('dp', None, 'heads')
Inputs may be any that keep to these rules, and one draw needn't show every extreme that they name: `seq_images`: every image is read by at least one and at most 12 entries, and some image by exactly 12. A sequence may name one image twice. `tile_count`: some image has 7 tiles and some has 1. `text_len`: some sequence has 128 tokens and some 128 // 2. `tile_mask`: tile 0 of every image that a sequence reads is 1.
All inputs are finite; a program needn't handle non-finite values.
Results may differ from a plain program's by a relative error of at most 0.012.
Values may be sent and summed in bfloat16 or wider, within the bound.
A program may use at most 64 MiB of HBM per device.

v0:
```python
from functools import reduce
import math

import jax
import jax.numpy as jnp
from jax import lax
from jax.sharding import PartitionSpec as P

D_HEAD = 128
Q_HEADS = 64
KV_HEADS = 8


score_rows = 512


def dot_rows(left_side, right_side):
    return lax.dot_general(
        left_side, right_side, (((1,), (1,)), ((), ())), preferred_element_type=jnp.float32
    )


def dot_cols(left_side, right_side):
    return lax.dot_general(
        left_side, right_side, (((0,), (0,)), ((), ())), preferred_element_type=jnp.float32
    )


def fetch_slots(keys, values, slot_of):
    held_keys, held_values = (
        lax.all_to_all(keys, "dp", split_axis=1, concat_axis=0, tiled=True),
        lax.all_to_all(values, "dp", split_axis=1, concat_axis=0, tiled=True),
    )
    order_map = jnp.transpose(slot_of)
    sent_keys = jnp.take(held_keys, order_map, axis=0)
    sent_values = jnp.take(held_values, order_map, axis=0)
    got_keys, got_values = (
        lax.all_to_all(sent_keys, "dp", split_axis=1, concat_axis=1, tiled=True),
        lax.all_to_all(sent_values, "dp", split_axis=1, concat_axis=1, tiled=True),
    )
    slots_read = slot_of.shape[1]
    width = got_keys.shape[-1]
    return (got_keys.reshape(slots_read, -1, width), got_values.reshape(slots_read, -1, width))


def masked_scores(query_rows, key_block, key_mask, score_scale):
    return jnp.where(key_mask[None, :], dot_rows(query_rows, key_block) * score_scale, -jnp.inf)


def forward_block(query_rows, key_reads, value_reads, key_ok, score_scale):
    peaks, masses, partials = ([], [], [])
    for slot_index in range(key_reads.shape[0]):
        scores = masked_scores(query_rows, key_reads[slot_index], key_ok[slot_index], score_scale)
        peak_score = jnp.max(scores, axis=1, keepdims=True)
        expos = jnp.exp(scores - peak_score)
        peaks.append(peak_score)
        masses.append(jnp.sum(expos, axis=1, keepdims=True))
        partials.append(
            jnp.dot(
                expos.astype(jnp.bfloat16),
                value_reads[slot_index],
                preferred_element_type=jnp.float32,
            )
        )
    top_peak = reduce(jnp.maximum, peaks)
    weights = [jnp.exp(peak_score - top_peak) for peak_score in peaks]
    total_mass = reduce(jnp.add, [weight * mass_part for weight, mass_part in zip(weights, masses)])
    mixture = (
        reduce(
            jnp.add, [weight * partial_value for weight, partial_value in zip(weights, partials)]
        )
        / total_mass
    )
    return (mixture, top_peak + jnp.log(total_mass))


def backward_block(
    query_rows, grad_rows, mixture, log_mass, key_reads, value_reads, key_ok, score_scale
):
    deltas = jnp.sum(grad_rows.astype(jnp.float32) * mixture, axis=1, keepdims=True)
    query_grad = jnp.zeros(mixture.shape, jnp.float32)
    key_parts, value_parts = ([], [])
    for slot_index in range(key_reads.shape[0]):
        scores = masked_scores(query_rows, key_reads[slot_index], key_ok[slot_index], score_scale)
        probs = jnp.exp(scores - log_mass)
        value_parts.append(dot_cols(probs.astype(jnp.bfloat16), grad_rows))
        dprobs = dot_rows(grad_rows, value_reads[slot_index])
        dscores = (probs * (dprobs - deltas) * score_scale).astype(jnp.bfloat16)
        query_grad = query_grad + jnp.dot(
            dscores, key_reads[slot_index], preferred_element_type=jnp.float32
        )
        key_parts.append(dot_cols(dscores, query_rows))
    return (query_grad, jnp.stack(key_parts), jnp.stack(value_parts))


def return_grads(key_part, value_part, slot_of):
    slots_read, key_rows, width = key_part.shape
    holders = lax.axis_size("dp")
    piece_rows = key_rows // holders
    back_keys, back_values = (
        lax.all_to_all(
            key_part.reshape(slots_read, holders, piece_rows, width),
            "dp",
            split_axis=1,
            concat_axis=1,
            tiled=True,
        ),
        lax.all_to_all(
            value_part.reshape(slots_read, holders, piece_rows, width),
            "dp",
            split_axis=1,
            concat_axis=1,
            tiled=True,
        ),
    )
    owner_ids = jnp.arange(holders, dtype=jnp.int32)
    select = (jnp.transpose(slot_of)[None, :, :] == owner_ids[:, None, None]).astype(jnp.bfloat16)
    summed_keys = jnp.einsum("ojr,jrpf->opf", select, back_keys, preferred_element_type=jnp.float32)
    summed_values = jnp.einsum(
        "ojr,jrpf->opf", select, back_values, preferred_element_type=jnp.float32
    )
    home_keys, home_values = (
        lax.all_to_all(
            summed_keys.astype(jnp.bfloat16), "dp", split_axis=0, concat_axis=1, tiled=True
        ),
        lax.all_to_all(
            summed_values.astype(jnp.bfloat16), "dp", split_axis=0, concat_axis=1, tiled=True
        ),
    )
    return (home_keys, home_values)


def on_device(
    queries, out_grad, keys, values, image_owner, tile_count, seq_images, text_len, tile_mask
):
    query_local, grad_local = (
        lax.all_to_all(queries, "heads", split_axis=2, concat_axis=1, tiled=True),
        lax.all_to_all(out_grad, "heads", split_axis=2, concat_axis=1, tiled=True),
    )
    length = query_local.shape[1]
    kv_local = keys.shape[2] // D_HEAD
    group_size = Q_HEADS // KV_HEADS
    per_block = max(1, min(group_size, score_rows // length))
    splits = group_size // per_block
    blocks = kv_local * splits
    block_rows = length * per_block
    score_scale = 1.0 / math.sqrt(D_HEAD)
    image_ids = jnp.arange(tile_count.shape[0], dtype=jnp.int32)
    matches = seq_images[:, :, None] == image_ids[None, None, :]
    slot_of = jnp.sum(jnp.where(matches, image_owner[None, None, :], 0), axis=2)
    device_index = lax.axis_index("dp")
    my_matches = lax.dynamic_slice_in_dim(matches, device_index, 1, 0)[0]
    counts = jnp.sum(jnp.where(my_matches, tile_count[None, :], 0), axis=1)
    tiles = tile_mask.shape[2]
    tile_rows = keys.shape[1] // tiles
    tile_ok = (jnp.arange(tiles)[None, :] < counts[:, None]) & (tile_mask[0] == 1)
    key_ok = jnp.repeat(tile_ok, tile_rows, axis=1)
    token_ok = (jnp.arange(length) < text_len[0]).astype(jnp.float32)
    row_ok = jnp.repeat(token_ok, per_block)[:, None]
    view_shape = (length, kv_local, splits, per_block, D_HEAD)
    query_view = query_local[0].reshape(view_shape)
    grad_view = (grad_local[0] * token_ok[:, None].astype(jnp.bfloat16)).reshape(view_shape)

    def rows_of(view, block_index):
        head_index = block_index // splits
        part_index = block_index % splits
        taken = lax.dynamic_slice(
            view, (0, head_index, part_index, 0, 0), (length, 1, 1, per_block, D_HEAD)
        )
        return taken.reshape(block_rows, D_HEAD)

    def put_rows(view, rows_in, block_index):
        head_index = block_index // splits
        part_index = block_index % splits
        return lax.dynamic_update_slice(
            view,
            rows_in.reshape(length, 1, 1, per_block, D_HEAD),
            (0, head_index, part_index, 0, 0),
        )

    key_reads, value_reads = fetch_slots(keys, values, slot_of)

    def forward_step(block_index, loop_state):
        mixture_view, log_all = loop_state
        mixture, log_mass = forward_block(
            rows_of(query_view, block_index), key_reads, value_reads, key_ok, score_scale
        )
        mixture = mixture * row_ok
        return (
            put_rows(mixture_view, mixture, block_index),
            lax.dynamic_update_index_in_dim(log_all, log_mass, block_index, 0),
        )

    mixture_view, log_all = lax.fori_loop(
        0,
        blocks,
        forward_step,
        (jnp.zeros(view_shape, jnp.float32), jnp.zeros((blocks, block_rows, 1), jnp.float32)),
    )
    key_back, value_back = (key_reads, value_reads)

    def backward_step(block_index, loop_state):
        qgrad_view, key_acc, value_acc = loop_state
        log_mass = lax.dynamic_index_in_dim(log_all, block_index, 0, keepdims=False)
        query_grad, key_part, value_part = backward_block(
            rows_of(query_view, block_index),
            rows_of(grad_view, block_index),
            rows_of(mixture_view, block_index),
            log_mass,
            key_back,
            value_back,
            key_ok,
            score_scale,
        )
        offset = block_index // splits * D_HEAD
        key_acc = lax.dynamic_update_slice_in_dim(key_acc, key_acc + key_part, offset, 2)
        value_acc = lax.dynamic_update_slice_in_dim(value_acc, value_acc + value_part, offset, 2)
        return (
            put_rows(qgrad_view, query_grad.astype(jnp.bfloat16), block_index),
            key_acc,
            value_acc,
        )

    zeros_acc = jnp.zeros(key_reads.shape, jnp.float32)
    qgrad_view, key_acc, value_acc = lax.fori_loop(
        0, blocks, backward_step, (jnp.zeros(view_shape, jnp.bfloat16), zeros_acc, zeros_acc)
    )
    key_grad, value_grad = return_grads(
        key_acc.astype(jnp.bfloat16), value_acc.astype(jnp.bfloat16), slot_of
    )
    attn_local = mixture_view.astype(jnp.bfloat16).reshape(1, length, -1)
    qgrad_local = qgrad_view.reshape(1, length, -1)
    attn_out, query_grad = (
        lax.all_to_all(attn_local, "heads", split_axis=1, concat_axis=2, tiled=True),
        lax.all_to_all(qgrad_local, "heads", split_axis=1, concat_axis=2, tiled=True),
    )
    return (attn_out, query_grad, key_grad, value_grad)


def solution(mesh):
    in_specs = (
        P("dp", "heads", None),
        P("dp", "heads", None),
        P("dp", None, "heads"),
        P("dp", None, "heads"),
        P(),
        P(),
        P(),
        P("dp"),
        P("dp", None, None),
    )
    out_specs = (
        P("dp", "heads", None),
        P("dp", "heads", None),
        P("dp", None, "heads"),
        P("dp", None, "heads"),
    )
    return jax.shard_map(
        on_device, mesh=mesh, in_specs=in_specs, out_specs=out_specs, check_vma=False
    )
```

profile of v0, /device:TPU:1, one launch (start us, length us, event | category | flops | bytes accessed | tf_op | source)
XLA Modules:
  0.0 585.2 jit_solution(13503863506161010646)
XLA Ops:
  5.9 10.1 %reduce.21 = bf16[1792,128]{1,0:T(8,128)(2,1)S(1)} reduce(bf16[1792,1,128]{2,1,0:T(2,128)(2,1)S(1)} %bitcast.256, bf16[]{:T(256)} %broadcast.89), dimensions={1}, to_apply=%bitcast.153.reduce_sub_computation | reduce | bytes 917506
  17.0 19.5 %all-to-all-start.1 = ((bf16[64,2,1792]{2,1,0:T(2,128)(2,1)}), bf16[64,2,1792]{2,1,0:T(2,128)(2,1)S(1)}, u32[]{:S(2)}, u32[]{:S(2)}) async-start(bf16[64,2,1792]{2,1,0:T(2,128)(2,1)} %reshape.320), calls=%async_computation.1 | async-start | bytes 917504 | tf_op jit(solution)/shard_map/all_to_all | solution.py:31
  43.6 10.1 %reduce.20 = bf16[1792,128]{1,0:T(8,128)(2,1)S(1)} reduce(bf16[1792,1,128]{2,1,0:T(2,128)(2,1)S(1)} %bitcast.257, bf16[]{:T(256)} %broadcast.89), dimensions={1}, to_apply=%bitcast.152.reduce_sub_computation | reduce | bytes 917506
  54.6 8.7 %all-to-all-done.1 = bf16[64,2,1792]{2,1,0:T(2,128)(2,1)S(1)} async-done(((bf16[64,2,1792]{2,1,0:T(2,128)(2,1)}), bf16[64,2,1792]{2,1,0:T(2,128)(2,1)S(1)}, u32[]{:S(2)}, u32[]{:S(2)}) %all-to-all-start.1) | async-done | bytes 458784 | tf_op jit(solution)/shard_map/all_to_all | solution.py:31
  63.3 8.6 %all-to-all-start.3 = ((bf16[64,2,1792]{2,1,0:T(2,128)(2,1)}), bf16[64,2,1792]{2,1,0:T(2,128)(2,1)S(1)}, u32[]{:S(2)}, u32[]{:S(2)}) async-start(bf16[64,2,1792]{2,1,0:T(2,128)(2,1)} %reshape.322), calls=%async_computation.3 | async-start | bytes 917504 | tf_op jit(solution)/shard_map/all_to_all | solution.py:32
  80.1 45.2 %reduce.19 = bf16[8192,16]{1,0:T(8,128)(2,1)S(1)} reduce(bf16[8192,1,16]{2,1,0:T(2,128)(2,1)} %bitcast.248, bf16[]{:T(256)} %broadcast.89), dimensions={1}, to_apply=%bitcast.118.reduce_sub_computation | reduce | bytes 524290
  134.8 45.6 %reduce.23 = bf16[8192,16]{1,0:T(8,128)(2,1)S(1)} reduce(bf16[8192,1,16]{2,1,0:T(2,128)(2,1)} %bitcast.249, bf16[]{:T(256)} %broadcast.89), dimensions={1}, to_apply=%bitcast.126.reduce_sub_computation | reduce | bytes 524290
  218.6 59.5 %all_to_all.134 = bf16[2,64,28,128]{3,0,2,1:T(2,128)(2,1)} all-to-all(bf16[2,64,28,128]{3,0,2,1:T(2,128)(2,1)S(1)} %get-tuple-element.691), channel_id=1, replica_groups=mesh['dp'=64,'heads'=8] {'dp'}, dimensions={1} | all-to-all | bytes 1835008 | tf_op jit(solution)/shard_map/all_to_all | solution.py:39
  278.1 10.2 %all-to-all-start.2 = ((bf16[2,64,28,128]{3,0,2,1:T(2,128)(2,1)}), bf16[2,64,28,128]{3,0,2,1:T(2,128)(2,1)S(1)}, u32[]{:S(2)}, u32[]{:S(2)}) async-start(bf16[2,64,28,128]{3,0,2,1:T(2,128)(2,1)} %get-tuple-element.692), calls=%async_computation.2 | async-start | bytes 1835008 | tf_op jit(solution)/shard_map/all_to_all | solution.py:38
  294.5 7.9 %copy.123 = bf16[1,16,8192]{2,1,0:T(8,128)(2,1)S(1)} copy(bf16[1,16,8192]{1,0,2:T(2,128)(2,1)} %bitcast.246) | data formatting | bytes 524288 | tf_op jit(solution)/shard_map/all_to_all | solution.py:137
  309.2 7.9 %copy.138 = bf16[1,16,8192]{2,1,0:T(8,128)(2,1)S(1)} copy(bf16[1,16,8192]{1,0,2:T(2,128)(2,1)} %bitcast.247) | data formatting | bytes 524288 | tf_op jit(solution)/shard_map/all_to_all | solution.py:138
  319.1 14.1 %all-to-all-done.2 = bf16[2,64,28,128]{3,0,2,1:T(2,128)(2,1)S(1)} async-done(((bf16[2,64,28,128]{3,0,2,1:T(2,128)(2,1)}), bf16[2,64,28,128]{3,0,2,1:T(2,128)(2,1)S(1)}, u32[]{:S(2)}, u32[]{:S(2)}) %all-to-all-start.2) | async-done | bytes 917536 | tf_op jit(solution)/shard_map/all_to_all | solution.py:38
  335.5 9.1 %while.38 = (s32[]{:T(128)}, f32[128,1,2,4,128]{4,3,0,2,1:T(4,128)S(1)}, f32[2,512,1]{1,2,0:T(1,128)S(1)}, pred[2,1792]{1,0:T(4,128)(4,1)S(1)}, bf16[128,1,2,4,1...) while((s32[]{:T(128)}, ...), condition=%wide.region_7.9_spmd.clone, body=%wide.region_2.8_spmd.clone.sunk | while | flops 952701440 | bytes 25757404 | solution.py:194
  349.8 8.1 %all-to-all-start.5 = ((bf16[8,2,8192]{2,1,0:T(2,128)(2,1)}), bf16[8,2,8192]{2,1,0:T(2,128)(2,1)S(1)}, u32[]{:S(2)}, u32[]{:S(2)}) async-start(bf16[8,2,8192]{2,1,0:T(2,128)(2,1)} %reshape.324), calls=%async_computation.5 | async-start | bytes 524288 | tf_op jit(solution)/shard_map/all_to_all | solution.py:234
  358.7 24.0 %while.39 = (s32[]{:T(128)}, bf16[128,1,2,4,128]{0,4,3,2,1:T(8,128)(2,1)}, f32[2,1792,128]{2,1,0:T(8,128)}, f32[2,1792,128]{2,1,0:T(8,128)}, pred[2,1792]{1,0:T(...) while((s32[]{:T(128)}, ...), condition=%wide.region_10.12_spmd.clone, body=%wide.region_8.11_spmd.clone.sunk | while | flops 2366569984 | bytes 82998656 | solution.py:225
  392.4 8.4 %copy.152 = bf16[2,1792,128]{2,0,1:T(2,128)(2,1)} copy(bf16[2,1792,128]{2,1,0:T(8,128)(2,1)S(1)} %convert_element_type.117) | data formatting | bytes 1835008 | tf_op jit(solution)/shard_map/convert_element_type | solution.py:229
  407.3 8.4 %copy.149 = bf16[2,1792,128]{2,0,1:T(2,128)(2,1)} copy(bf16[2,1792,128]{2,1,0:T(8,128)(2,1)S(1)} %convert_element_type.115) | data formatting | bytes 1835008 | tf_op jit(solution)/shard_map/convert_element_type | solution.py:229
  415.6 37.3 %all-to-all-done.10 = bf16[2,64,28,128]{3,0,2,1:T(2,128)(2,1)S(1)} async-done(((bf16[2,64,28,128]{3,0,2,1:T(2,128)(2,1)}), bf16[2,64,28,128]{3,0,2,1:T(2,128)(2,1)S(1)}, u32[]{:S(2)}, u32[]{:S(2)}) %all-to-all-start.10) | async-done | bytes 917536 | tf_op jit(solution)/shard_map/all_to_all | solution.py:108
  452.9 9.3 %all-to-all-start.8 = ((bf16[2,64,28,128]{3,0,2,1:T(2,128)(2,1)}), bf16[2,64,28,128]{3,0,2,1:T(2,128)(2,1)S(1)}, u32[]{:S(2)}, u32[]{:S(2)}) async-start(bf16[2,64,28,128]{3,0,2,1:T(2,128)(2,1)} %bitcast.18), calls=%async_computation.8 | async-start | bytes 1835008 | tf_op jit(solution)/shard_map/all_to_all | solution.py:101
  463.8 43.9 %all-to-all-done.8 = bf16[2,64,28,128]{3,0,2,1:T(2,128)(2,1)S(1)} async-done(((bf16[2,64,28,128]{3,0,2,1:T(2,128)(2,1)}), bf16[2,64,28,128]{3,0,2,1:T(2,128)(2,1)S(1)}, u32[]{:S(2)}, u32[]{:S(2)}) %all-to-all-start.8) | async-done | bytes 917536 | tf_op jit(solution)/shard_map/all_to_all | solution.py:101
  507.7 9.4 %all-to-all-start.11 = ((bf16[64,28,128]{2,1,0:T(8,128)(2,1)}), bf16[64,28,128]{2,1,0:T(8,128)(2,1)S(1)}, u32[]{:S(2)}, u32[]{:S(2)}) async-start(bf16[64,28,128]{2,1,0:T(8,128)(2,1)} %copy.154), calls=%async_computation.11 | async-start | bytes 1048576 | tf_op jit(solution)/shard_map/all_to_all | solution.py:126
  518.6 27.6 %all-to-all-done.11 = bf16[64,28,128]{2,1,0:T(8,128)(2,1)S(1)} async-done(((bf16[64,28,128]{2,1,0:T(8,128)(2,1)}), bf16[64,28,128]{2,1,0:T(8,128)(2,1)S(1)}, u32[]{:S(2)}, u32[]{:S(2)}) %all-to-all-start.11) | async-done | bytes 458784 | tf_op jit(solution)/shard_map/all_to_all | solution.py:126
  546.2 8.9 %all-to-all-start.9 = ((bf16[64,28,128]{2,1,0:T(8,128)(2,1)}), bf16[64,28,128]{2,1,0:T(8,128)(2,1)S(1)}, u32[]{:S(2)}, u32[]{:S(2)}) async-start(bf16[64,28,128]{2,1,0:T(8,128)(2,1)} %copy.151), calls=%async_computation.9 | async-start | bytes 1048576 | tf_op jit(solution)/shard_map/all_to_all | solution.py:123
  558.1 26.0 %all-to-all-done.9 = bf16[64,28,128]{2,1,0:T(8,128)(2,1)S(1)} async-done(((bf16[64,28,128]{2,1,0:T(8,128)(2,1)}), bf16[64,28,128]{2,1,0:T(8,128)(2,1)S(1)}, u32[]{:S(2)}, u32[]{:S(2)}) %all-to-all-start.9) | async-done | bytes 458784 | tf_op jit(solution)/shard_map/all_to_all | solution.py:123
  (178 shorter events, 148.2 us)
Async XLA Ops:
  0.6 35.8 %copy-start.7 = (bf16[1,1792,128]{2,1,0:T(8,128)(2,1)S(1)}, bf16[1,1792,128]{2,1,0:T(8,128)(2,1)}, u32[]{:S(2)}) copy-start(bf16[1,1792,128]{2,1,0:T(8,128)(2,1)} %param.18) | copy-start | bytes 1376260
  5.9 66.0 %copy-start.10 = (s32[64,2]{0,1:T(2,128)S(1)}, s32[64,2]{0,1:T(2,128)}, u32[]{:S(2)}) copy-start(s32[64,2]{0,1:T(2,128)} %param.21) | copy-start | bytes 1540
  5.9 66.1 %copy-start.12 = (s32[64]{0:T(128)S(1)}, s32[64]{0:T(128)}, u32[]{:S(2)}) copy-start(s32[64]{0:T(128)} %param.19) | copy-start | bytes 772
  5.9 67.5 %copy-start.8 = (bf16[1,16,8192]{2,1,0:T(8,128)(2,1)S(1)}, bf16[1,16,8192]{2,1,0:T(8,128)(2,1)}, u32[]{:S(2)}) copy-start(bf16[1,16,8192]{2,1,0:T(8,128)(2,1)} %param.15) | copy-start | bytes 786436
  17.0 46.3 %all-to-all-start.1 = ((bf16[64,2,1792]{2,1,0:T(2,128)(2,1)}), bf16[64,2,1792]{2,1,0:T(2,128)(2,1)S(1)}, u32[]{:S(2)}, u32[]{:S(2)}) async-start(bf16[64,2,1792]{2,1,0:T(2,128)(2,1)} %reshape.320), calls=%async_computation.1 | async-start | bytes 917504 | tf_op jit(solution)/shard_map/all_to_all | solution.py:31
  63.3 120.4 %all-to-all-start.3 = ((bf16[64,2,1792]{2,1,0:T(2,128)(2,1)}), bf16[64,2,1792]{2,1,0:T(2,128)(2,1)S(1)}, u32[]{:S(2)}, u32[]{:S(2)}) async-start(bf16[64,2,1792]{2,1,0:T(2,128)(2,1)} %reshape.322), calls=%async_computation.3 | async-start | bytes 917504 | tf_op jit(solution)/shard_map/all_to_all | solution.py:32
  80.1 48.0 %copy-start.9 = (bf16[1,16,8192]{2,1,0:T(8,128)(2,1)S(1)}, bf16[1,16,8192]{2,1,0:T(8,128)(2,1)}, u32[]{:S(2)}) copy-start(bf16[1,16,8192]{2,1,0:T(8,128)(2,1)} %param.16) | copy-start | bytes 786436
  183.7 23.5 %all-to-all-start = ((bf16[8,2,8192]{2,1,0:T(2,128)(2,1)}), bf16[8,2,8192]{2,1,0:T(2,128)(2,1)S(1)}, u32[]{:S(2)}, u32[]{:S(2)}) async-start(bf16[8,2,8192]{2,1,0:T(2,128)(2,1)} %reshape.318), calls=%async_computation | async-start | bytes 524288 | tf_op jit(solution)/shard_map/all_to_all | solution.py:137
  207.1 11.4 %all-to-all-start.6 = ((bf16[8,2,8192]{2,1,0:T(2,128)(2,1)}), bf16[8,2,8192]{2,1,0:T(2,128)(2,1)}, u32[]{:S(2)}, u32[]{:S(2)}) async-start(bf16[8,2,8192]{2,1,0:T(2,128)(2,1)} %reshape.326), calls=%async_computation.6 | async-start | bytes 524288 | tf_op jit(solution)/shard_map/all_to_all | solution.py:138
  211.9 77.1 %copy-start.13 = (s32[64]{0:T(128)S(1)}, s32[64]{0:T(128)}, u32[]{:S(2)}) copy-start(s32[64]{0:T(128)} %param.20) | copy-start | bytes 772
  211.9 77.3 %copy-start.11 = (s32[1,2,7]{2,1,0:T(2,128)S(1)}, s32[1,2,7]{2,1,0:T(2,128)}, u32[]{:S(2)}) copy-start(s32[1,2,7]{2,1,0:T(2,128)} %param.23) | copy-start | bytes 172
  278.1 55.1 %all-to-all-start.2 = ((bf16[2,64,28,128]{3,0,2,1:T(2,128)(2,1)}), bf16[2,64,28,128]{3,0,2,1:T(2,128)(2,1)S(1)}, u32[]{:S(2)}, u32[]{:S(2)}) async-start(bf16[2,64,28,128]{3,0,2,1:T(2,128)(2,1)} %get-tuple-element.692), calls=%async_computation.2 | async-start | bytes 1835008 | tf_op jit(solution)/shard_map/all_to_all | solution.py:38
  349.8 37.4 %all-to-all-start.5 = ((bf16[8,2,8192]{2,1,0:T(2,128)(2,1)}), bf16[8,2,8192]{2,1,0:T(2,128)(2,1)S(1)}, u32[]{:S(2)}, u32[]{:S(2)}) async-start(bf16[8,2,8192]{2,1,0:T(2,128)(2,1)} %reshape.324), calls=%async_computation.5 | async-start | bytes 524288 | tf_op jit(solution)/shard_map/all_to_all | solution.py:234
  364.4 2.0 copy-start
  364.4 2.0 copy-start.3
  376.4 2.0 copy-start
  376.4 2.0 copy-start.3
  382.8 9.5 %copy-start.2 = (f32[2,1792,128]{2,1,0:T(8,128)S(1)}, f32[2,1792,128]{2,1,0:T(8,128)}, u32[]{:S(2)}) copy-start(f32[2,1792,128]{2,1,0:T(8,128)} %get-tuple-element.476) | copy-start | bytes 5505028
  387.2 13.6 %all-to-all-start.7 = ((bf16[8,2,8192]{2,1,0:T(2,128)(2,1)}), bf16[8,2,8192]{2,1,0:T(2,128)(2,1)S(1)}, u32[]{:S(2)}, u32[]{:S(2)}) async-start(bf16[8,2,8192]{2,1,0:T(2,128)(2,1)} %reshape.328), calls=%async_computation.7 | async-start | bytes 524288 | tf_op jit(solution)/shard_map/all_to_all | solution.py:235
  392.4 14.7 %copy-start.5 = (f32[2,1792,128]{2,1,0:T(8,128)S(1)}, f32[2,1792,128]{2,1,0:T(8,128)}, u32[]{:S(2)}) copy-start(f32[2,1792,128]{2,1,0:T(8,128)} %get-tuple-element.475) | copy-start | bytes 5505028
  400.8 52.1 %all-to-all-start.10 = ((bf16[2,64,28,128]{3,0,2,1:T(2,128)(2,1)}), bf16[2,64,28,128]{3,0,2,1:T(2,128)(2,1)S(1)}, u32[]{:S(2)}, u32[]{:S(2)}) async-start(bf16[2,64,28,128]{3,0,2,1:T(2,128)(2,1)} %bitcast.21), calls=%async_computation.10 | async-start | bytes 1835008 | tf_op jit(solution)/shard_map/all_to_all | solution.py:108
  452.9 54.8 %all-to-all-start.8 = ((bf16[2,64,28,128]{3,0,2,1:T(2,128)(2,1)}), bf16[2,64,28,128]{3,0,2,1:T(2,128)(2,1)S(1)}, u32[]{:S(2)}, u32[]{:S(2)}) async-start(bf16[2,64,28,128]{3,0,2,1:T(2,128)(2,1)} %bitcast.18), calls=%async_computation.8 | async-start | bytes 1835008 | tf_op jit(solution)/shard_map/all_to_all | solution.py:101
  507.7 38.5 %all-to-all-start.11 = ((bf16[64,28,128]{2,1,0:T(8,128)(2,1)}), bf16[64,28,128]{2,1,0:T(8,128)(2,1)S(1)}, u32[]{:S(2)}, u32[]{:S(2)}) async-start(bf16[64,28,128]{2,1,0:T(8,128)(2,1)} %copy.154), calls=%async_computation.11 | async-start | bytes 1048576 | tf_op jit(solution)/shard_map/all_to_all | solution.py:126
  546.2 37.9 %all-to-all-start.9 = ((bf16[64,28,128]{2,1,0:T(8,128)(2,1)}), bf16[64,28,128]{2,1,0:T(8,128)(2,1)S(1)}, u32[]{:S(2)}, u32[]{:S(2)}) async-start(bf16[64,28,128]{2,1,0:T(8,128)(2,1)} %copy.151), calls=%async_computation.9 | async-start | bytes 1048576 | tf_op jit(solution)/shard_map/all_to_all | solution.py:123
  (5 other events, 5.9 us)
where the time goes:
time: 595 us; the launch traced here: 585 us
  waiting for transfers between devices  161 us (27%)
  other arithmetic  126 us (21%)
  local copies, waits for them, and re-layouts  119 us (20%)
  starting transfers between devices  96.3 us (16%)
  blocking collectives  59.5 us (10%)
  matrix products  20.7 us (3%)
    unnamed x9, other arithmetic  116 us
    all_to_all x1, blocking collectives, fetch_slots(): lax.all_to_all(sent_values, 'dp', split_axis=1, concat_axis=1, tiled=True)  59.5 us
    unnamed x46, local copies, waits for them, and re-layouts  51.9 us
    all_to_all x1, waiting for transfers between devices, return_grads(): lax.all_to_all(key_part.reshape(slots_read, holders, piece_rows, width),...  43.9 us
    all_to_all x1, waiting for transfers between devices, return_grads(): lax.all_to_all(value_part.reshape(slots_read, holders, piece_rows, width)...  37.3 us
    all_to_all x1, waiting for transfers between devices, return_grads(): lax.all_to_all(summed_values.astype(jnp.bfloat16), 'dp', split_axis=0, co...  27.6 us
    all_to_all x1, waiting for transfers between devices, return_grads(): lax.all_to_all(summed_keys.astype(jnp.bfloat16), 'dp', split_axis=0, conc...  26 us
    all_to_all x1, starting transfers between devices, fetch_slots(): lax.all_to_all(keys, 'dp', split_axis=1, concat_axis=0, tiled=True)  19.5 us
  transfers between devices with their start and end apart: 11, of which 7 were waited for; matrix products, arithmetic and copies ran while one was open for 39% of the time, Pallas kernels for 0%

commit v1 on v0

v1 whole, which is shorter than its diff:
```python
import functools
import math

import jax
import jax.numpy as jnp
from jax import lax
from jax.experimental import pallas as pl
from jax.experimental.pallas import tpu as pltpu
from jax.sharding import PartitionSpec as P

D_HEAD = 128
NY = 4
NZ = 16
NH = 8
TILES = 7
READS = 2
BLOCK = 16
TEXT = 128
GROUP = 8
ROWS = TEXT * GROUP
WIDTH = GROUP * D_HEAD
SLOTS = NY * NZ
UNITS = READS * TILES
MESH = pl.DeviceIdType.MESH
VMEM_BYTES = 56 * 1024 * 1024


def far_first(step):
    half = step // 2
    return jnp.where(lax.rem(step, 2) == 1, 8 + half, 8 - half)


def place():
    me = lax.axis_index("dp")
    return me, me // NZ, lax.rem(me, NZ), lax.axis_index("heads")


def greet_all():
    me, my, mz, mh = place()
    barrier = pltpu.get_barrier_semaphore()

    def greet(device):
        pl.semaphore_signal(barrier, inc=1, device_id=device, device_id_type=MESH)

    def greet_z(step, carry):
        greet((my * NZ + lax.rem(mz + step, NZ), mh))
        return carry

    def greet_y(step, carry):
        greet((lax.rem(my + step, NY) * NZ + mz, mh))
        return carry

    def greet_h(step, carry):
        greet((me, lax.rem(mh + step, NH)))
        return carry

    lax.fori_loop(1, NZ, greet_z, 0)
    lax.fori_loop(1, NY, greet_y, 0)
    lax.fori_loop(1, NH, greet_h, 0)
    pl.semaphore_wait(barrier, NZ + NY + NH - 3)


def loop(start, stop, step_of):
    def body(step, carry):
        step_of(step)
        return carry

    lax.fori_loop(start, stop, body, 0)


def fetch_kernel(
    slots, q, g, k, v, q_out, g_out, k_out, v_out,
    held_k, held_v, send_k, send_v,
    head_send, head_recv, a_send, a_recv, b_send, b_recv, c_send, c_recv, local_sem,
):
    me, my, mz, mh = place()
    greet_all()
    sides = ((k, held_k, send_k, k_out), (v, held_v, send_v, v_out))

    def scatter(side, step):
        to = lax.rem(mz + far_first(step), NZ)
        return pltpu.make_async_remote_copy(
            src_ref=sides[side][0].at[:, to],
            dst_ref=sides[side][1].at[me],
            send_sem=a_send.at[side, to],
            recv_sem=a_recv.at[side, mz],
            device_id=(my * NZ + to, mh),
            device_id_type=MESH,
        )

    def scattered(side, source):
        return pltpu.make_async_remote_copy(
            src_ref=sides[side][0].at[:, source],
            dst_ref=sides[side][1].at[my * NZ + source],
            send_sem=a_send.at[side, source],
            recv_sem=a_recv.at[side, source],
            device_id=(my * NZ + source, mh),
            device_id_type=MESH,
        )

    def keep(side):
        return pltpu.make_async_copy(
            sides[side][0].at[:, mz], sides[side][1].at[me], local_sem.at[side]
        )

    def exchange(which, step):
        src, dst = ((q, q_out), (g, g_out))[which]
        to = lax.rem(mh + step, NH)
        return pltpu.make_async_remote_copy(
            src_ref=src.at[:, pl.ds(pl.multiple_of(to * WIDTH, WIDTH), WIDTH)],
            dst_ref=dst.at[mh],
            send_sem=head_send.at[which, to],
            recv_sem=head_recv.at[which, mh],
            device_id=(me, to),
            device_id_type=MESH,
        )

    def exchanged(which, step):
        src, dst = ((q, q_out), (g, g_out))[which]
        source = lax.rem(mh + step, NH)
        return pltpu.make_async_remote_copy(
            src_ref=src.at[:, pl.ds(pl.multiple_of(source * WIDTH, WIDTH), WIDTH)],
            dst_ref=dst.at[source],
            send_sem=head_send.at[which, source],
            recv_sem=head_recv.at[which, source],
            device_id=(me, source),
            device_id_type=MESH,
        )

    def own(which):
        src, dst = ((q, q_out), (g, g_out))[which]
        return pltpu.make_async_copy(
            src.at[:, pl.ds(pl.multiple_of(mh * WIDTH, WIDTH), WIDTH)],
            dst.at[mh],
            local_sem.at[2 + which],
        )

    def share(side, source, step):
        to = lax.rem(my + step, NY)
        return pltpu.make_async_remote_copy(
            src_ref=sides[side][1].at[my * NZ + source],
            dst_ref=sides[side][1].at[my * NZ + source],
            send_sem=b_send.at[side, to, source],
            recv_sem=b_recv.at[side, my, source],
            device_id=(to * NZ + mz, mh),
            device_id_type=MESH,
        )

    def shared(side, source, step):
        origin = lax.rem(my + step, NY)
        return pltpu.make_async_remote_copy(
            src_ref=sides[side][1].at[origin * NZ + source],
            dst_ref=sides[side][1].at[origin * NZ + source],
            send_sem=b_send.at[side, origin, source],
            recv_sem=b_recv.at[side, origin, source],
            device_id=(origin * NZ + mz, mh),
            device_id_type=MESH,
        )

    def deliver(side, to):
        return pltpu.make_async_remote_copy(
            src_ref=sides[side][2].at[to],
            dst_ref=sides[side][3].at[mz],
            send_sem=c_send.at[side, to],
            recv_sem=c_recv.at[side, mz],
            device_id=(my * NZ + to, mh),
            device_id_type=MESH,
        )

    def delivered(side, source):
        return pltpu.make_async_remote_copy(
            src_ref=sides[side][2].at[source],
            dst_ref=sides[side][3].at[source],
            send_sem=c_send.at[side, source],
            recv_sem=c_recv.at[side, source],
            device_id=(my * NZ + source, mh),
            device_id_type=MESH,
        )

    def deliver_own(side):
        return pltpu.make_async_copy(
            sides[side][2].at[mz], sides[side][3].at[mz], local_sem.at[4 + side]
        )

    for side in range(2):
        keep(side).start()
        loop(1, NZ, lambda step: scatter(side, step).start())
    for which in range(2):
        own(which).start()
        loop(1, NH, lambda step: exchange(which, step).start())

    def pass_on(side):
        keep(side).wait()
        loop(1, NY, lambda step: share(side, mz, step).start())

        def forward(step):
            source = lax.rem(mz + far_first(step), NZ)
            scattered(side, source).wait_recv()
            loop(1, NY, lambda turn: share(side, source, turn).start())

        loop(1, NZ, forward)

    def send_reads(side):
        held, send = sides[side][1], sides[side][2]
        loop(1, NY, lambda turn: loop(0, NZ, lambda source: shared(side, source, turn).wait_recv()))

        def gather(to):
            for read in range(READS):
                slot = slots[(my * NZ + to) * READS + read]
                send[to, read] = held[slot]

        def one(step):
            to = lax.rem(mz + far_first(step), NZ)
            gather(to)
            deliver(side, to).start()

        loop(1, NZ, one)
        gather(mz)
        deliver_own(side).start()

    pass_on(0)
    send_reads(0)
    pass_on(1)
    send_reads(1)

    for which in range(2):
        own(which).wait()
        loop(1, NH, lambda step: exchanged(which, step).wait_recv())
        loop(1, NH, lambda step: exchange(which, step).wait_send())
    for side in range(2):
        deliver_own(side).wait()
        loop(1, NZ, lambda step: scatter(side, step).wait_send())
        loop(1, NY, lambda turn: loop(0, NZ, lambda source: share(side, source, turn).wait_send()))
        loop(1, NZ, lambda step: delivered(side, lax.rem(mz + step, NZ)).wait_recv())
        loop(1, NZ, lambda step: deliver(side, lax.rem(mz + step, NZ)).wait_send())


def fetch(slots, q, g, k, v):
    any_spec = pl.BlockSpec(memory_space=pl.ANY)
    part = (TILES, BLOCK, D_HEAD)
    dma = pltpu.SemaphoreType.DMA
    return pl.pallas_call(
        fetch_kernel,
        out_shape=(
            jax.ShapeDtypeStruct((NH, TEXT // NH, WIDTH), jnp.bfloat16),
            jax.ShapeDtypeStruct((NH, TEXT // NH, WIDTH), jnp.bfloat16),
            jax.ShapeDtypeStruct((NZ, READS) + part, jnp.bfloat16),
            jax.ShapeDtypeStruct((NZ, READS) + part, jnp.bfloat16),
        ),
        in_specs=[pl.BlockSpec(memory_space=pltpu.SMEM)] + [any_spec] * 4,
        out_specs=(any_spec,) * 4,
        scratch_shapes=[
            pltpu.VMEM((SLOTS,) + part, jnp.bfloat16),
            pltpu.VMEM((SLOTS,) + part, jnp.bfloat16),
            pltpu.VMEM((NZ, READS) + part, jnp.bfloat16),
            pltpu.VMEM((NZ, READS) + part, jnp.bfloat16),
            dma((2, NH)), dma((2, NH)),
            dma((2, NZ)), dma((2, NZ)),
            dma((2, NY, NZ)), dma((2, NY, NZ)),
            dma((2, NZ)), dma((2, NZ)),
            dma((6,)),
        ],
        compiler_params=pltpu.CompilerParams(
            collective_id=1, has_side_effects=True, vmem_limit_bytes=VMEM_BYTES
        ),
        name="fetch",
    )(slots, q, g, k, v)


def attend_kernel(
    order, facts, q, g, k, v, attn, q_grad, k_grad, v_grad,
    q_rows, g_rows, q_cols, g_cols, scores,
):
    active = facts[0]
    length = facts[1]
    scale = 1.0 / math.sqrt(D_HEAD)
    token = lax.broadcasted_iota(jnp.int32, (TEXT, D_HEAD), 0)
    for head in range(GROUP):
        lanes = slice(head * D_HEAD, (head + 1) * D_HEAD)
        rows = slice(head * TEXT, (head + 1) * TEXT)
        q_head = q[:, lanes]
        g_head = jnp.where(token < length, g[:, lanes].astype(jnp.float32), 0.0)
        q_rows[rows, :] = q_head
        g_rows[rows, :] = g_head.astype(jnp.bfloat16)
        q_cols[:, rows] = jnp.transpose(q_head.astype(jnp.float32)).astype(jnp.bfloat16)
        g_cols[:, rows] = jnp.transpose(g_head).astype(jnp.bfloat16)

    def tile_of(ref, unit):
        return ref[:, unit].reshape(NZ * BLOCK, D_HEAD)

    def nn(left, right):
        return jnp.dot(left, right, preferred_element_type=jnp.float32)

    def tn(left, right):
        return lax.dot_general(
            left, right, (((0,), (0,)), ((), ())), preferred_element_type=jnp.float32
        )

    def score_step(index, peak):
        unit = order[index]
        part = nn(tile_of(k, unit), q_cols[...])
        scores[unit] = part
        return jnp.maximum(peak, jnp.max(part, axis=0, keepdims=True))

    peak = lax.fori_loop(
        0, active, score_step, jnp.full((1, ROWS), -jnp.inf, jnp.float32)
    )
    peak_scaled = peak * scale

    def mix_step(index, state):
        mass, mixed = state
        unit = order[index]
        expo = jnp.exp(scores[unit] * scale - peak_scaled)
        scores[unit] = expo
        mass = mass + jnp.sum(expo, axis=0, keepdims=True)
        mixed = mixed + tn(tile_of(v, unit), expo.astype(jnp.bfloat16))
        return mass, mixed

    mass, mixed = lax.fori_loop(
        0,
        active,
        mix_step,
        (jnp.zeros((1, ROWS), jnp.float32), jnp.zeros((D_HEAD, ROWS), jnp.float32)),
    )
    inverse = 1.0 / mass
    column = lax.rem(lax.broadcasted_iota(jnp.int32, (1, ROWS), 1), TEXT)
    mixture = mixed * jnp.where(column < length, inverse, 0.0)
    delta = jnp.sum(mixture * g_cols[...].astype(jnp.float32), axis=0, keepdims=True)
    for head in range(GROUP):
        lanes = slice(head * D_HEAD, (head + 1) * D_HEAD)
        attn[:, lanes] = jnp.transpose(mixture[:, lanes]).astype(jnp.bfloat16)

    def back_step(index, q_total):
        unit = order[index]
        probs = scores[unit] * inverse
        v_grad[:, unit] = (
            nn(probs.astype(jnp.bfloat16), g_rows[...])
            .astype(jnp.bfloat16)
            .reshape(NZ, BLOCK, D_HEAD)
        )
        inner = nn(tile_of(v, unit), g_cols[...])
        dscores = (probs * ((inner - delta) * scale)).astype(jnp.bfloat16)
        k_grad[:, unit] = (
            nn(dscores, q_rows[...]).astype(jnp.bfloat16).reshape(NZ, BLOCK, D_HEAD)
        )
        return q_total + tn(tile_of(k, unit), dscores)

    q_total = lax.fori_loop(0, active, back_step, jnp.zeros((D_HEAD, ROWS), jnp.float32))
    for head in range(GROUP):
        lanes = slice(head * D_HEAD, (head + 1) * D_HEAD)
        q_grad[:, lanes] = jnp.transpose(q_total[:, lanes]).astype(jnp.bfloat16)

    def clear_step(index, carry):
        unit = order[index]
        nothing = jnp.zeros((NZ, BLOCK, D_HEAD), jnp.bfloat16)
        k_grad[:, unit] = nothing
        v_grad[:, unit] = nothing
        return carry

    lax.fori_loop(active, UNITS, clear_step, 0)


def attend(order, facts, q, g, k, v):
    smem = pl.BlockSpec(memory_space=pltpu.SMEM)
    vmem = pl.BlockSpec(memory_space=pltpu.VMEM)
    reads = (NZ, UNITS, BLOCK, D_HEAD)
    return pl.pallas_call(
        attend_kernel,
        out_shape=(
            jax.ShapeDtypeStruct((TEXT, WIDTH), jnp.bfloat16),
            jax.ShapeDtypeStruct((TEXT, WIDTH), jnp.bfloat16),
            jax.ShapeDtypeStruct(reads, jnp.bfloat16),
            jax.ShapeDtypeStruct(reads, jnp.bfloat16),
        ),
        in_specs=[smem, smem] + [vmem] * 4,
        out_specs=(vmem,) * 4,
        scratch_shapes=[
            pltpu.VMEM((ROWS, D_HEAD), jnp.bfloat16),
            pltpu.VMEM((ROWS, D_HEAD), jnp.bfloat16),
            pltpu.VMEM((D_HEAD, ROWS), jnp.bfloat16),
            pltpu.VMEM((D_HEAD, ROWS), jnp.bfloat16),
            pltpu.VMEM((UNITS, NZ * BLOCK, ROWS), jnp.float32),
        ],
        compiler_params=pltpu.CompilerParams(vmem_limit_bytes=VMEM_BYTES),
        name="attend",
    )(order, facts, q.reshape(TEXT, WIDTH), g.reshape(TEXT, WIDTH), k.reshape(reads), v.reshape(reads))


def give_kernel(
    order, same, last, has, attn, q_grad, k_part, v_part,
    attn_out, q_out, k_out, v_out,
    back_k, back_v, run, row_k, row_v, col_k, col_v, sum_k, sum_v,
    head_send, head_recv, a_send, a_recv, b_send, b_recv, c_send, c_recv, local_sem,
):
    me, my, mz, mh = place()
    greet_all()
    sides = (
        (v_part, back_v, row_v, col_v, sum_v, v_out),
        (k_part, back_k, row_k, col_k, sum_k, k_out),
    )

    def give(side, to):
        return pltpu.make_async_remote_copy(
            src_ref=sides[side][0].at[pl.ds(to * READS, READS)],
            dst_ref=sides[side][1].at[pl.ds(mz * READS, READS)],
            send_sem=c_send.at[side, to],
            recv_sem=c_recv.at[side, mz],
            device_id=(my * NZ + to, mh),
            device_id_type=MESH,
        )

    def given(side, source):
        return pltpu.make_async_remote_copy(
            src_ref=sides[side][0].at[pl.ds(source * READS, READS)],
            dst_ref=sides[side][1].at[pl.ds(source * READS, READS)],
            send_sem=c_send.at[side, source],
            recv_sem=c_recv.at[side, source],
            device_id=(my * NZ + source, mh),
            device_id_type=MESH,
        )

    def give_own(side):
        return pltpu.make_async_copy(
            sides[side][0].at[pl.ds(mz * READS, READS)],
            sides[side][1].at[pl.ds(mz * READS, READS)],
            local_sem.at[side],
        )

    def exchange(which, to):
        src, dst = ((attn, attn_out), (q_grad, q_out))[which]
        return pltpu.make_async_remote_copy(
            src_ref=src.at[to],
            dst_ref=dst.at[:, pl.ds(pl.multiple_of(mh * WIDTH, WIDTH), WIDTH)],
            send_sem=head_send.at[which, to],
            recv_sem=head_recv.at[which, mh],
            device_id=(me, to),
            device_id_type=MESH,
        )

    def exchanged(which, source):
        src, dst = ((attn, attn_out), (q_grad, q_out))[which]
        return pltpu.make_async_remote_copy(
            src_ref=src.at[source],
            dst_ref=dst.at[:, pl.ds(pl.multiple_of(source * WIDTH, WIDTH), WIDTH)],
            send_sem=head_send.at[which, source],
            recv_sem=head_recv.at[which, source],
            device_id=(me, source),
            device_id_type=MESH,
        )

    def own(which):
        src, dst = ((attn, attn_out), (q_grad, q_out))[which]
        return pltpu.make_async_copy(
            src.at[mh],
            dst.at[:, pl.ds(pl.multiple_of(mh * WIDTH, WIDTH), WIDTH)],
            local_sem.at[2 + which],
        )

    def hand(side, step):
        to = lax.rem(my + step, NY)
        return pltpu.make_async_remote_copy(
            src_ref=sides[side][2].at[pl.ds(to * NZ, NZ)],
            dst_ref=sides[side][3].at[my],
            send_sem=b_send.at[side, to],
            recv_sem=b_recv.at[side, my],
            device_id=(to * NZ + mz, mh),
            device_id_type=MESH,
        )

    def handed(side, step):
        source = lax.rem(my + step, NY)
        return pltpu.make_async_remote_copy(
            src_ref=sides[side][2].at[pl.ds(source * NZ, NZ)],
            dst_ref=sides[side][3].at[source],
            send_sem=b_send.at[side, source],
            recv_sem=b_recv.at[side, source],
            device_id=(source * NZ + mz, mh),
            device_id_type=MESH,
        )

    def bring(side, to):
        return pltpu.make_async_remote_copy(
            src_ref=sides[side][4].at[to],
            dst_ref=sides[side][5].at[:, mz],
            send_sem=a_send.at[side, to],
            recv_sem=a_recv.at[side, mz],
            device_id=(my * NZ + to, mh),
            device_id_type=MESH,
        )

    def brought(side, source):
        return pltpu.make_async_remote_copy(
            src_ref=sides[side][4].at[source],
            dst_ref=sides[side][5].at[:, source],
            send_sem=a_send.at[side, source],
            recv_sem=a_recv.at[side, source],
            device_id=(my * NZ + source, mh),
            device_id_type=MESH,
        )

    def bring_own(side):
        return pltpu.make_async_copy(
            sides[side][4].at[mz], sides[side][5].at[:, mz], local_sem.at[4 + side]
        )

    for side in range(2):
        give_own(side).start()
        loop(1, NZ, lambda step: give(side, lax.rem(mz + far_first(step), NZ)).start())
    for which in range(2):
        own(which).start()
        loop(1, NH, lambda step: exchange(which, lax.rem(mh + step, NH)).start())

    def sum_reads(side):
        back, row = sides[side][1], sides[side][2]
        give_own(side).wait()
        loop(1, NZ, lambda step: given(side, lax.rem(mz + step, NZ)).wait_recv())
        run[0] = back[order[0]].astype(jnp.float32)

        def add(step):
            weight = same[step].astype(jnp.float32)
            run[step] = run[step - 1] * weight + back[order[step]].astype(jnp.float32)

        loop(1, NZ * READS, add)

        def pick(slot):
            weight = has[slot].astype(jnp.float32)
            row[slot] = (run[last[slot]] * weight).astype(jnp.bfloat16)

        loop(0, SLOTS, pick)
        loop(1, NY, lambda step: hand(side, step).start())

    def sum_columns(side):
        row, col, total = sides[side][2], sides[side][3], sides[side][4]
        loop(1, NY, lambda step: handed(side, step).wait_recv())

        def one(to):
            acc = row[my * NZ + to].astype(jnp.float32)
            for step in range(1, NY):
                acc = acc + col[lax.rem(my + step, NY), to].astype(jnp.float32)
            total[to] = acc.astype(jnp.bfloat16)

        def one_sent(step):
            to = lax.rem(mz + far_first(step), NZ)
            one(to)
            bring(side, to).start()

        loop(1, NZ, one_sent)
        one(mz)
        bring_own(side).start()

    sum_reads(0)
    sum_columns(0)
    sum_reads(1)
    sum_columns(1)

    for which in range(2):
        own(which).wait()
        loop(1, NH, lambda step: exchanged(which, lax.rem(mh + step, NH)).wait_recv())
        loop(1, NH, lambda step: exchange(which, lax.rem(mh + step, NH)).wait_send())
    for side in range(2):
        loop(1, NZ, lambda step: give(side, lax.rem(mz + step, NZ)).wait_send())
        loop(1, NY, lambda step: hand(side, step).wait_send())
        bring_own(side).wait()
        loop(1, NZ, lambda step: brought(side, lax.rem(mz + step, NZ)).wait_recv())
        loop(1, NZ, lambda step: bring(side, lax.rem(mz + step, NZ)).wait_send())


def give_back(order, same, last, has, attn, q_grad, k_part, v_part):
    any_spec = pl.BlockSpec(memory_space=pl.ANY)
    part = (TILES, BLOCK, D_HEAD)
    dma = pltpu.SemaphoreType.DMA
    bf16 = jnp.bfloat16
    return pl.pallas_call(
        give_kernel,
        out_shape=(
            jax.ShapeDtypeStruct((TEXT // NH, NH * WIDTH), bf16),
            jax.ShapeDtypeStruct((TEXT // NH, NH * WIDTH), bf16),
            jax.ShapeDtypeStruct((TILES, NZ, BLOCK, D_HEAD), bf16),
            jax.ShapeDtypeStruct((TILES, NZ, BLOCK, D_HEAD), bf16),
        ),
        in_specs=[pl.BlockSpec(memory_space=pltpu.SMEM)] * 4 + [any_spec] * 4,
        out_specs=(any_spec,) * 4,
        scratch_shapes=[
            pltpu.VMEM((NZ * READS,) + part, bf16),
            pltpu.VMEM((NZ * READS,) + part, bf16),
            pltpu.VMEM((NZ * READS,) + part, jnp.float32),
            pltpu.VMEM((SLOTS,) + part, bf16),
            pltpu.VMEM((SLOTS,) + part, bf16),
            pltpu.VMEM((NY, NZ) + part, bf16),
            pltpu.VMEM((NY, NZ) + part, bf16),
            pltpu.VMEM((NZ,) + part, bf16),
            pltpu.VMEM((NZ,) + part, bf16),
            dma((2, NH)), dma((2, NH)),
            dma((2, NZ)), dma((2, NZ)),
            dma((2, NY)), dma((2, NY)),
            dma((2, NZ)), dma((2, NZ)),
            dma((6,)),
        ],
        compiler_params=pltpu.CompilerParams(
            collective_id=2, has_side_effects=True, vmem_limit_bytes=VMEM_BYTES
        ),
        name="give_back",
    )(
        order, same, last, has,
        attn.reshape(NH, TEXT // NH, WIDTH), q_grad.reshape(NH, TEXT // NH, WIDTH),
        k_part.reshape((NZ * READS,) + part), v_part.reshape((NZ * READS,) + part),
    )


def on_device(
    queries, out_grad, keys, values, image_owner, tile_count, seq_images, text_len, tile_mask
):
    images = tile_count.shape[0]
    device_index = lax.axis_index("dp")
    matches = seq_images.reshape(-1)[:, None] == jnp.arange(images, dtype=jnp.int32)[None, :]
    slot_of = jnp.sum(jnp.where(matches, image_owner[None, :], 0), axis=1)
    counts = jnp.sum(jnp.where(matches, tile_count[None, :], 0), axis=1)

    my_counts = lax.dynamic_slice_in_dim(counts, device_index * READS, READS, 0)
    units = jnp.arange(UNITS, dtype=jnp.int32)
    tile_ok = (
        (jnp.arange(TILES, dtype=jnp.int32)[None, :] < my_counts[:, None]) & (tile_mask[0] == 1)
    ).reshape(-1)
    sort_key = jnp.where(tile_ok, units, units + UNITS)
    rank = jnp.sum((sort_key[None, :] < sort_key[:, None]).astype(jnp.int32), axis=1)
    unit_order = jnp.sum(jnp.where(rank[None, :] == units[:, None], units[None, :], 0), axis=1)
    facts = jnp.stack([jnp.sum(tile_ok.astype(jnp.int32)), text_len[0]])

    row_reads = NZ * READS
    row_slots = lax.dynamic_slice_in_dim(slot_of, device_index // NZ * row_reads, row_reads, 0)
    reads = jnp.arange(row_reads, dtype=jnp.int32)
    read_key = row_slots * row_reads + reads
    read_rank = jnp.sum((read_key[None, :] < read_key[:, None]).astype(jnp.int32), axis=1)
    placed = read_rank[None, :] == reads[:, None]
    read_order = jnp.sum(jnp.where(placed, reads[None, :], 0), axis=1)
    sorted_slots = jnp.sum(jnp.where(placed, row_slots[None, :], 0), axis=1)
    same = jnp.concatenate(
        [jnp.zeros((1,), jnp.int32), (sorted_slots[1:] == sorted_slots[:-1]).astype(jnp.int32)]
    )
    slot_ids = jnp.arange(SLOTS, dtype=jnp.int32)
    up_to = jnp.sum((row_slots[None, :] <= slot_ids[:, None]).astype(jnp.int32), axis=1)
    has = jnp.max((row_slots[None, :] == slot_ids[:, None]).astype(jnp.int32), axis=1)
    last = jnp.maximum(up_to - 1, 0)

    split = (TILES, NZ, BLOCK, D_HEAD)
    q_heads, g_heads, k_reads, v_reads = fetch(
        slot_of, queries[0], out_grad[0], keys.reshape(split), values.reshape(split)
    )
    attn, q_grad, k_part, v_part = attend(unit_order, facts, q_heads, g_heads, k_reads, v_reads)
    attn_out, query_grad, key_grad, value_grad = give_back(
        read_order, same, last, has, attn, q_grad, k_part, v_part
    )
    return (
        attn_out[None],
        query_grad[None],
        key_grad.reshape(keys.shape),
        value_grad.reshape(values.shape),
    )


def solution(mesh):
    in_specs = (
        P("dp", "heads", None),
        P("dp", "heads", None),
        P("dp", None, "heads"),
        P("dp", None, "heads"),
        P(),
        P(),
        P(),
        P("dp"),
        P("dp", None, None),
    )
    out_specs = (
        P("dp", "heads", None),
        P("dp", "heads", None),
        P("dp", None, "heads"),
        P("dp", None, "heads"),
    )
    return jax.shard_map(
        on_device, mesh=mesh, in_specs=in_specs, out_specs=out_specs, check_vma=False
    )
```

time: 595 us -> 307 us (0.52); the launches traced: 585 us -> 307 us
  Pallas kernels: 0 us -> 293 us
  waiting for transfers between devices: 161 us -> 0 us
  other arithmetic: 126 us -> 5.69 us
  local copies, waits for them, and re-layouts: 119 us -> 6.68 us
  starting transfers between devices: 96.3 us -> 0 us
  blocking collectives: 59.5 us -> 0 us
  matrix products: 20.7 us -> 0 us
    pallas_call x0 -> x3, Pallas kernels: none -> 293 us  [the longest x1 140 us: fetch(): pl.pallas_call(fetch_kernel, out_shape=(jax.ShapeDtypeStruct((NH, TEXT //...]
    all_to_all x11 -> x0, waiting for transfers between devices: 161 us -> none  [the longest x1 43.9 us: return_grads(): lax.all_to_all(key_part.reshape(slots_read, holders, piece_rows, width),...]
    unnamed x9 -> x0, other arithmetic: 116 us -> none
    all_to_all x11 -> x0, starting transfers between devices: 96.3 us -> none  [the longest x1 19.5 us: fetch_slots(): lax.all_to_all(keys, 'dp', split_axis=1, concat_axis=0, tiled=True)]
    all_to_all x1 -> x0, blocking collectives: 59.5 us -> none  [fetch_slots(): lax.all_to_all(sent_values, 'dp', split_axis=1, concat_axis=1, tiled=True)]
    unnamed x46 -> x21, local copies, waits for them, and re-layouts: 51.9 us -> 6.29 us
    all_to_all x14 -> x0, local copies, waits for them, and re-layouts: 34.7 us -> none  [the longest x3 8.03 us: on_device(): lax.all_to_all(queries, 'heads', split_axis=2, concat_axis=1, tiled=True)]
    dot_general x30 -> x0, matrix products: 20.7 us -> none  [the longest x12 9.08 us: dot_rows(): lax.dot_general(left_side, right_side, (((1,), (1,)), ((), ())), preferre...]
  transfers between devices with their start and end apart: 11 -> 0, of which waited for: 7 -> 0; matrix products, arithmetic and copies ran while one was open for 39% -> 0% of each run, Pallas kernels for 0% -> 0%
where the time goes in v1:
time: 307 us
  Pallas kernels  293 us (95%)
  local copies, waits for them, and re-layouts  6.68 us (2%)
  other arithmetic  5.69 us (2%)
    pallas_call x1, Pallas kernels, fetch(): pl.pallas_call(fetch_kernel, out_shape=(jax.ShapeDtypeStruct((NH, TEXT //...  140 us
    pallas_call x1, Pallas kernels, give_back(): pl.pallas_call(give_kernel, out_shape=(jax.ShapeDtypeStruct((TEXT // NH,...  137 us
    pallas_call x1, Pallas kernels, attend(): pl.pallas_call(attend_kernel, out_shape=(jax.ShapeDtypeStruct((TEXT, WIDT...  16.9 us
    unnamed x21, local copies, waits for them, and re-layouts  6.29 us

profile of v1, /device:TPU:1, one launch (start us, length us, event | category | flops | bytes accessed | tf_op | source)
XLA Modules:
  0.0 306.9 jit_solution(9804697825394112966)
XLA Ops:
  1.3 0.7 copy-done.4
  2.0 0.1 copy.15
  2.1 0.1 eq.72
  2.2 0.5 copy-done.6
  2.7 0.1 select_reduce_fusion
  3.0 0.1 lt.66
  3.1 0.6 copy-done.5
  3.7 0.7 fusion.1
  4.5 0.2 convert_reduce_fusion.3
  4.7 0.7 select_reduce_fusion.4.order
  5.4 1.2 pad_add_fusion.facts
  6.7 0.2 convert_reduce_fusion.2
  6.9 0.6 select_reduce_fusion.2
  7.6 0.6 add_convert_fusion.same
  8.2 0.6 convert_reduce_fusion
  8.8 0.5 add_maximum_fusion.last
  9.3 139.6 %fetch.1 = (bf16[8,16,1024]{2,1,0:T(8,128)(2,1)}, bf16[8,16,1024]{2,1,0:T(8,128)(2,1)}, bf16[16,2,7,16,128]{4,3,2,1,0:T(8,128)(2,1)}, bf16[16,2,7,16,128]{4,3,2,1,0:T(8,128)(2,1)}) custom-call(s32[128]{0:T(128)} %copy-done.3, bf16[16,8192]{1,0:T(8,128)(2,1)} %bitcast.35, bf16[16,8192]{1,0:T(8,128)(2,1)} %bitcast.36, bf16[7,16,16,128]{3,2,1,0:T(8,128)(2,1)} %bitcast.29, ...), custom_call_target="tpu_custom_call" | custom-call | tf_op jit(solution)/shard_map/fetch/pallas_call | solution.py:242
  148.9 16.9 %attend.1 = (bf16[128,1024]{1,0:T(8,128)(2,1)}, bf16[128,1024]{1,0:T(8,128)(2,1)}, bf16[16,14,16,128]{3,2,1,0:T(8,128)(2,1)}, bf16[16,14,16,128]{3,2,1,0:T(8,128)(2,1)}) custom-call(s32[14]{0:T(128)} %select_reduce_fusion.4.order, s32[2]{0:T(128)} %pad_add_fusion.facts, bf16[128,1024]{1,0:T(8,128)(2,1)} %bitcast.31, bf16[128,1024]{1,0:T(8,128)(2,1)} %bitcast.32, ...), custom_call_target="tpu_custom_call" | custom-call | tf_op jit(solution)/shard_map/attend/pallas_call | solution.py:367
  165.9 136.6 %give_back.1 = (bf16[16,8192]{1,0:T(8,128)(2,1)}, bf16[16,8192]{1,0:T(8,128)(2,1)}, bf16[7,16,16,128]{3,2,1,0:T(8,128)(2,1)}, bf16[7,16,16,128]{3,2,1,0:T(8,128)(2,1)}) custom-call(s32[32]{0:T(128)} %get-tuple-element.33.order, s32[32]{0:T(128)} %add_convert_fusion.same, s32[64]{0:T(128)} %add_maximum_fusion.last, s32[64]{0:T(128)} %get-tuple-element.30.has, ...), custom_call_target="tpu_custom_call" | custom-call | tf_op jit(solution)/shard_map/give_back/pallas_call | solution.py:573
  302.5 1.7 copy.21
  304.3 0.7 copy.22
  305.0 0.8 copy.23
  305.7 0.4 copy-done
  306.1 0.8 copy.24
  (18 shorter events, 0.4 us)
Async XLA Ops:
  1.3 0.7 copy-start.4
  2.1 0.7 copy-start.6
  2.1 0.7 copy-start.7
  2.8 3.8 %copy-start.3 = (s32[128]{0:T(128)}, s32[128]{0:T(128)S(1)}, u32[]{:S(2)}) copy-start(s32[128]{0:T(128)S(1)} %get-tuple-element.29.slots) | copy-start | bytes 1540
  3.0 0.7 copy-start.5
  302.5 1.8 copy-start.2
  302.5 2.5 copy-start.1
  305.0 1.2 copy-start
